TPU v7x, 512 devices: a whole 4x4x16 slice. The times are simulated.
512 devices in a mesh: grp: 8 (over x, y_hi), chan: 64 (over y_lo, z, core).
Axes of the slice: x: 4, y: 4 (y_hi: 2, y_lo: 2; y = y_hi * 2 + y_lo), z: 16, core: 2. Of those that a mesh axis runs over, the one named last changes fastest.
Arguments:
- voltages: bfloat16 [512, 1024, 1024], P('grp', 'chan'), may hold values from -6 to 6
- prototype: float32 [8, 1024], replicated, may hold values from -2 to 2
Outputs:
- visibilities: float32 [8, 5, 512, 2, 64, 64], P('grp', None, 'chan')
All inputs are finite; a program needn't handle non-finite values.
Results may differ from a plain program's by a relative error of at most 0.0033.
Values may be sent and summed in bfloat16 or wider, within the bound.
A program may use at most 64 MiB of HBM per device.

v0:
```python
import math

import jax
import jax.numpy as jnp
from jax import lax
from jax.sharding import PartitionSpec as P


def from_behind(value, axis, by):
    devices = lax.axis_size(axis)
    pairs = [(i, i + by) for i in range(devices) if 0 <= i + by < devices]
    return lax.ppermute(value, axis, pairs)


def passed_along(value, axis, steps):
    count = lax.axis_size(axis)
    pairs = [(source, (source + steps) % count) for source in range(count)]
    return lax.ppermute(value, axis, pairs)


def dft_table(frame_len, chan_count):
    sample = jnp.arange(frame_len, dtype=jnp.int32)[:, None]
    channel = jnp.arange(chan_count, dtype=jnp.int32)[None, :]
    phase = (sample * channel % frame_len).astype(jnp.float32) * (2.0 * math.pi / frame_len)
    scaling = 1.0 / math.sqrt(frame_len)
    table = jnp.stack([jnp.cos(phase) * scaling, -jnp.sin(phase) * scaling], axis=2)
    return table.reshape(frame_len, 2 * chan_count).astype(jnp.bfloat16)


def shards(voltages, prototype):
    tap_count = prototype.shape[0]
    spec_dev = voltages.shape[1]
    frame_len = voltages.shape[2]
    earlier = from_behind(voltages[:, spec_dev - (tap_count - 1) :, :], "chan", 1)
    joined = jnp.concatenate([earlier, voltages], axis=1)
    filtered = jnp.zeros(voltages.shape, jnp.float32)
    for offset in range(tap_count):
        filtered = filtered + prototype[offset][None, None, :] * joined[
            :, offset : offset + spec_dev, :
        ].astype(jnp.float32)
    filtered = filtered.astype(jnp.bfloat16)
    table = dft_table(frame_len, frame_len // 2)
    spectra = jnp.einsum("isn,nq->qsi", filtered, table, preferred_element_type=jnp.float32).astype(
        jnp.bfloat16
    )
    turned = lax.all_to_all(spectra, "chan", split_axis=0, concat_axis=1, tiled=True)
    chan_dev = turned.shape[0] // 2
    total_spec = turned.shape[1]
    width = turned.shape[2]
    blocks = turned.reshape(chan_dev, 2, total_spec, width)
    flipped = jnp.stack([blocks[:, 1], -blocks[:, 0]], axis=1)
    scaling = 1.0 / math.sqrt(total_spec)

    def correlate(partner):
        real_part = jnp.einsum(
            "cpsi,cpsj->cij", blocks, partner, preferred_element_type=jnp.float32
        )
        imag_part = jnp.einsum(
            "cpsi,cpsj->cij", flipped, partner, preferred_element_type=jnp.float32
        )
        return jnp.stack([real_part, imag_part], axis=1) * scaling

    group_count = lax.axis_size("grp")
    lag_count = group_count // 2 + 1
    results = [correlate(blocks)]
    current = blocks
    for lag in range(1, lag_count):
        current = passed_along(current, "grp", 1)
        results.append(correlate(current))
    return jnp.stack(results, axis=0)[None]


def solution(mesh):
    in_specs = (P("grp", "chan", None), P())
    out_specs = P("grp", None, "chan", None, None, None)
    return jax.shard_map(shards, mesh=mesh, in_specs=in_specs, out_specs=out_specs, check_vma=False)
```

profile of v0, /device:TPU:32, one launch (start us, length us, event | category | flops | bytes accessed | tf_op | source)
XLA Modules:
  0.0 389.0 jit_solution(11476385067521477640)
XLA Ops:
  0.0 1.5 slice.55
  2.1 1.9 collective-permute-start
  4.0 8.6 %multiply_convert_fusion = (bf16[1024,512,1]{1,0,2:T(8,128)(2,1)S(1)}, bf16[1024,512,1]{1,0,2:T(8,128)(2,1)S(1)}) fusion(), kind=kLoop, calls=%fused_computation.32 | loop fusion | flops 9961472 | bytes 2097152 | tf_op jit(solution)/shard_map/convert.1
  12.8 3.9 %copy.38 = bf16[1024,512,2]{0,2,1:T(2,128)(2,1)} copy(bf16[1024,512,2]{1,0,2:T(8,128)(2,1)S(1)} %pad_maximum_fusion.1) | data formatting | bytes 4194304 | tf_op jit(solution)/shard_map/stack | solution.py:26
  16.8 4.3 %convert_element_type.54 = bf16[1024,1024]{0,1:T(8,128)(2,1)} reshape(bf16[1024,512,2]{0,2,1:T(2,128)(2,1)} %copy.38) | data formatting | bytes 4194304 | tf_op jit(solution)/shard_map/convert_element_type | solution.py:27
  21.0 1.7 copy.40
  22.8 5.8 %add_convert_fusion = bf16[64,16,1024]{2,1,0:T(8,128)(2,1)S(1)} fusion(bf16[64,16,1024]{2,1,0:T(8,128)(2,1)S(1)} %copy-done.1, bf16[64,7,1024]{2,1,0:T(8,128)(2,1)S(1)} %copy.40, f32[1024]{0:T(1024)S(1)} %bitcast.102, f32[1024]{0:T(1024)S(1)} %bitcast.103, f32[1024]{0:T(1024)S(1)} %bitcast.97, f32[1024]{0:T(1024)S(1)} %bitcast.98, f32[1024]{0:T(1024)S(1)} %bitcast.99, ...), kind=kLoop, calls=%fused_computation.6 | loop fusion | flops 47185920 | bytes 5144576 | tf_op jit(solution)/shard_map/convert_element_type | solution.py:41
  28.6 2.8 convert_bitcast_fusion
  31.3 4.9 %copy.43 = bf16[1024,16,64]{2,1,0:T(8,128)(2,1)} copy(bf16[1024,16,64]{0,2,1:T(8,128)(2,1)S(1)} %convert_bitcast_fusion) | data formatting | bytes 4194304 | tf_op jit(solution)/shard_map/convert_element_type | solution.py:43
  36.2 6.8 %reshape.258 = bf16[64,2,8192]{2,1,0:T(2,128)(2,1)S(1)} reshape(bf16[1024,16,64]{2,1,0:T(8,128)(2,1)} %copy.43) | data formatting | bytes 4194304
  43.1 114.0 %all_to_all.15 = bf16[64,2,8192]{2,1,0:T(2,128)(2,1)} all-to-all(bf16[64,2,8192]{2,1,0:T(2,128)(2,1)S(1)} %reshape.258), channel_id=1, replica_groups=mesh['grp'=8,'chan'=64] {'chan'}, dimensions={0} | all-to-all | bytes 4194304 | tf_op jit(solution)/shard_map/all_to_all | solution.py:46
  157.0 7.9 %reshape.259 = bf16[1024,16,64]{2,1,0:T(8,128)(2,1)} reshape(bf16[64,2,8192]{2,1,0:T(2,128)(2,1)} %all_to_all.15) | data formatting | bytes 4194304
  165.0 5.2 %copy.44 = bf16[16,64,16,64]{3,2,1,0:T(8,128)(2,1)} copy(bf16[16,64,16,64]{3,2,0,1:T(8,128)(2,1)} %bitcast.94) | data formatting | bytes 4194304 | tf_op jit(solution)/shard_map/all_to_all | solution.py:46
  170.2 3.5 copy.47
  173.8 5.1 %collective-permute-start.1 = (bf16[8,2,1024,64]{2,3,1,0:T(8,128)(2,1)S(1)}, bf16[8,2,1024,64]{2,3,1,0:T(8,128)(2,1)S(1)}, u32[]{:S(2)}, u32[]{:S(2)}) collective-permute-start(bf16[8,2,1024,64]{2,3,1,0:T(8,128)(2,1)S(1)} %copy.47), channel_id=1, source_target_pairs={{0,64},{64,128},{128,192},{192,256},{256,320},{320,384},{384,448},... | collective-permute-start | bytes 6291464 | tf_op jit(solution)/shard_map/ppermute | solution.py:18
  178.8 48.6 %collective-permute-done.1 = bf16[8,2,1024,64]{2,3,1,0:T(8,128)(2,1)S(1)} collective-permute-done((bf16[8,2,1024,64]{2,3,1,0:T(8,128)(2,1)S(1)}, bf16[8,2,1024,64]{2,3,1,0:T(8,128)(2,1)S(1)}, u32[]{:S(2)}, u32[]{:S(2)}) %collective-permute-start.1) | collective-permute-done | bytes 2097184 | tf_op jit(solution)/shard_map/ppermute | solution.py:18
  227.4 2.7 collective-permute-start.2
  230.1 50.8 %collective-permute-done.2 = bf16[8,2,1024,64]{2,3,1,0:T(8,128)(2,1)S(1)} collective-permute-done((bf16[8,2,1024,64]{2,3,1,0:T(8,128)(2,1)S(1)}, bf16[8,2,1024,64]{2,3,1,0:T(8,128)(2,1)S(1)}, u32[]{:S(2)}, u32[]{:S(2)}) %collective-permute-start.2) | collective-permute-done | bytes 2097184 | tf_op jit(solution)/shard_map/ppermute | solution.py:18
  280.9 1.9 collective-permute-start.3
  283.0 1.0 convolution_bitcast_fusion.4
  283.9 1.4 convolution_bitcast_fusion.5
  285.4 1.3 convolution_bitcast_fusion.3
  286.7 46.9 %collective-permute-done.3 = bf16[8,2,1024,64]{2,3,1,0:T(8,128)(2,1)S(1)} collective-permute-done((bf16[8,2,1024,64]{2,3,1,0:T(8,128)(2,1)S(1)}, bf16[8,2,1024,64]{2,3,1,0:T(8,128)(2,1)S(1)}, u32[]{:S(2)}, u32[]{:S(2)}) %collective-permute-start.3) | collective-permute-done | bytes 2097184 | tf_op jit(solution)/shard_map/ppermute | solution.py:18
  333.6 2.1 collective-permute-start.4
  335.7 0.7 convolution_bitcast_fusion.9
  337.2 1.3 convolution_bitcast_fusion.2
  338.5 0.7 convolution_bitcast_fusion.7
  339.2 1.3 convolution_bitcast_fusion.1
  340.5 44.8 %collective-permute-done.4 = bf16[8,2,1024,64]{2,3,1,0:T(8,128)(2,1)S(1)} collective-permute-done((bf16[8,2,1024,64]{2,3,1,0:T(8,128)(2,1)S(1)}, bf16[8,2,1024,64]{2,3,1,0:T(8,128)(2,1)S(1)}, u32[]{:S(2)}, u32[]{:S(2)}) %collective-permute-start.4) | collective-permute-done | bytes 2097184 | tf_op jit(solution)/shard_map/ppermute | solution.py:18
  385.3 1.3 convolution_bitcast_fusion
  386.6 0.7 convolution_bitcast_fusion.6
  387.4 1.7 copy.55
  (19 shorter events, 2.0 us)
Async XLA Ops:
  2.1 19.0 %collective-permute-start = (bf16[64,7,1024]{2,0,1:T(8,128)(2,1)S(1)}, bf16[64,7,1024]{2,0,1:T(8,128)(2,1)}, u32[]{:S(2)}, u32[]{:S(2)}) collective-permute-start(bf16[64,7,1024]{2,0,1:T(8,128)(2,1)S(1)} %copy.75), channel_id=1, source_target_pairs={{0,1},{1,2},{2,3},{3,4},{4,5},{5,6},{6,7},{7,8},{8,9},{9,10},{10,1... | collective-permute-start | bytes 2752520 | tf_op jit(solution)/shard_map/ppermute | solution.py:12
  16.8 4.3 %copy-start.3 = (f32[8,1024]{1,0:T(8,128)S(1)}, f32[8,1024]{1,0:T(8,128)}, u32[]{:S(2)}) copy-start(f32[8,1024]{1,0:T(8,128)} %param.3) | copy-start | bytes 98308
  16.8 6.0 %copy-start.1 = (bf16[64,16,1024]{2,1,0:T(8,128)(2,1)S(1)}, bf16[64,16,1024]{2,1,0:T(8,128)(2,1)}, u32[]{:S(2)}) copy-start(bf16[64,16,1024]{2,1,0:T(8,128)(2,1)} %param.2) | copy-start | bytes 6291460
  22.8 5.8 %copy-start.2 = (bf16[1024,1024]{0,1:T(8,128)(2,1)S(1)}, bf16[1024,1024]{0,1:T(8,128)(2,1)}, u32[]{:S(2)}) copy-start(bf16[1024,1024]{0,1:T(8,128)(2,1)} %convert_element_type.54) | copy-start | bytes 6291460
  173.7 109.2 %copy-start = (bf16[16,64,16,64]{3,2,1,0:T(8,128)(2,1)S(1)}, bf16[16,64,16,64]{3,2,1,0:T(8,128)(2,1)}, u32[]{:S(2)}) copy-start(bf16[16,64,16,64]{3,2,1,0:T(8,128)(2,1)} %copy.44) | copy-start | bytes 6291460
  173.8 53.7 %collective-permute-start.1 = (bf16[8,2,1024,64]{2,3,1,0:T(8,128)(2,1)S(1)}, bf16[8,2,1024,64]{2,3,1,0:T(8,128)(2,1)S(1)}, u32[]{:S(2)}, u32[]{:S(2)}) collective-permute-start(bf16[8,2,1024,64]{2,3,1,0:T(8,128)(2,1)S(1)} %copy.47), channel_id=1, source_target_pairs={{0,64},{64,128},{128,192},{192,256},{256,320},{320,384},{384,448},... | collective-permute-start | bytes 6291464 | tf_op jit(solution)/shard_map/ppermute | solution.py:18
  227.4 53.5 %collective-permute-start.2 = (bf16[8,2,1024,64]{2,3,1,0:T(8,128)(2,1)S(1)}, bf16[8,2,1024,64]{2,3,1,0:T(8,128)(2,1)S(1)}, u32[]{:S(2)}, u32[]{:S(2)}) collective-permute-start(bf16[8,2,1024,64]{2,3,1,0:T(8,128)(2,1)S(1)} %collective-permute-done.1), channel_id=1, source_target_pairs={{0,64},{64,128},{128,192},{192,256},{256,320},{320,384},{384,448},... | collective-permute-start | bytes 6291464 | tf_op jit(solution)/shard_map/ppermute | solution.py:18
  280.9 52.7 %collective-permute-start.3 = (bf16[8,2,1024,64]{2,3,1,0:T(8,128)(2,1)S(1)}, bf16[8,2,1024,64]{2,3,1,0:T(8,128)(2,1)S(1)}, u32[]{:S(2)}, u32[]{:S(2)}) collective-permute-start(bf16[8,2,1024,64]{2,3,1,0:T(8,128)(2,1)S(1)} %collective-permute-done.2), channel_id=1, source_target_pairs={{0,64},{64,128},{128,192},{192,256},{256,320},{320,384},{384,448},... | collective-permute-start | bytes 6291464 | tf_op jit(solution)/shard_map/ppermute | solution.py:18
  333.6 51.8 %collective-permute-start.4 = (bf16[8,2,1024,64]{2,3,1,0:T(8,128)(2,1)S(1)}, bf16[8,2,1024,64]{2,3,1,0:T(8,128)(2,1)S(1)}, u32[]{:S(2)}, u32[]{:S(2)}) collective-permute-start(bf16[8,2,1024,64]{2,3,1,0:T(8,128)(2,1)S(1)} %collective-permute-done.3), channel_id=1, source_target_pairs={{0,64},{64,128},{128,192},{192,256},{256,320},{320,384},{384,448},... | collective-permute-start | bytes 6291464 | tf_op jit(solution)/shard_map/ppermute | solution.py:18
where the time goes:
time: 390 us; the launch traced here: 389 us
  waiting for transfers between devices  191 us (49%)
  blocking collectives  114 us (29%)
  local copies, waits for them, and re-layouts  42.1 us (11%)
  other arithmetic  15.1 us (4%)
  starting transfers between devices  13.7 us (4%)
  matrix products  12.9 us (3%)
    ppermute x4, waiting for transfers between devices, passed_along(): return lax.ppermute(value, axis, pairs)  191 us
    all_to_all x1, blocking collectives, shards(): lax.all_to_all(spectra, 'chan', split_axis=0, concat_axis=1, tiled=True)  114 us
    unnamed x11, local copies, waits for them, and re-layouts  15.4 us
    ppermute x4, starting transfers between devices, passed_along(): return lax.ppermute(value, axis, pairs)  11.8 us
    another operation x1, other arithmetic  8.61 us
  transfers between devices with their start and end apart: 5, of which 4 were waited for; matrix products, arithmetic and copies ran while one was open for 7% of the time, Pallas kernels for 0%

commit v1 on v0

v1 whole, which is shorter than its diff:
```python
import math

import jax
import jax.numpy as jnp
import numpy as np
from jax import lax
from jax.experimental import pallas as pl
from jax.experimental.pallas import tpu as pltpu
from jax.sharding import PartitionSpec as P

MESH = pl.DeviceIdType.MESH
BF16, F32 = jnp.bfloat16, jnp.float32

TAPS, FRAME, INP, SPEC = 8, 1024, 64, 16
NZ, NM, NG, NL = 16, 32, 8, 5
BACK, AHEAD = 4, 3
ROLES = [8] + [s * r for r in range(7, 0, -1) for s in (1, -1)] + [0]
HUB = 3


def hub_of(role):
    return 0 if abs(role) < 2 else (HUB if role > 0 else -HUB)


SIDE_A = [r for r in ROLES if hub_of(r) == HUB and r != HUB]
SIDE_B = [r for r in ROLES if hub_of(r) == -HUB and r != -HUB]
SIDE_C = [r for r in ROLES if hub_of(r) == 0 and r != 0]


def dft_table():
    m = np.arange(NM)
    plane = np.arange(NZ)[:, None]
    chan = (((m // 2) % 2) * NZ + plane) * 2 + m % 2
    k = 8 * chan + m // 4
    phase = (k[:, :, None] * np.arange(FRAME)) % FRAME * (2.0 * np.pi / FRAME)
    table = np.stack([np.cos(phase), -np.sin(phase)], axis=1) / math.sqrt(FRAME)
    table = table.reshape(NZ, 2, NM // 2, 2, FRAME).transpose(0, 3, 1, 2, 4)
    return table.reshape(NZ, 2, NM, FRAME).astype(jnp.bfloat16)


def kernel(volt, proto, table, out, vt, hs, hr, filt, stage, sendp, recvp, za, zb, zc, pa, pb, qa, qb, fin, rr,
           hsem, hrsem, psem, prsem, zsem, zrsem, qsem, qrsem, rsem, rrsem):
    grp = lax.axis_index("grp")
    chan = lax.axis_index("chan")
    core = lax.rem(chan, 2)
    z = lax.rem(chan // 2, NZ)
    ylo = chan // (2 * NZ)
    mine = grp * 4 + ylo * 2 + core
    sgn = 1 - 2 * core

    def in_plane(m):
        return (m // 4, (lax.rem(m // 2, 2) * NZ + z) * 2 + lax.rem(m, 2))

    def in_column(offset):
        return (grp, (ylo * NZ + lax.rem(z + offset + 2 * NZ, NZ)) * 2 + core)

    after = (grp, lax.rem(chan + 1, 64))
    before = (grp, lax.rem(chan + 63, 64))
    beyond = (grp, lax.rem(chan + 63 + 2 * core, 64))

    barrier = pltpu.get_barrier_semaphore()

    @pl.loop(1, NM)
    def _(k):
        pl.semaphore_signal(barrier, inc=1, device_id=in_plane(lax.rem(mine + k, NM)), device_id_type=MESH)

    for d in (1, 2, 3, 4, 5):
        for s in (1, -1):
            pl.semaphore_signal(barrier, inc=1, device_id=in_column(s * d), device_id_type=MESH)
    pl.semaphore_signal(barrier, inc=1, device_id=beyond, device_id_type=MESH)

    @pl.loop(0, INP)
    def _(i):
        for nt in range(8):
            tile = volt[i, :, nt * 128:(nt + 1) * 128].astype(F32)
            vt[nt, pl.ds(BACK * INP + i, SPEC, stride=INP), :] = tile

    @pl.loop(0, 8)
    def _(nt):
        for n, f in enumerate([16, 17, 18, 19, 4, 5, 6]):
            hs[n, nt] = vt[nt, f * INP:(f + 1) * INP, :].astype(BF16)

    pl.semaphore_wait(barrier, NM - 1 + 11)
    forward = pltpu.make_async_remote_copy(
        src_ref=hs.at[0:BACK], dst_ref=hr.at[0:BACK], send_sem=hsem.at[0], recv_sem=hrsem.at[0],
        device_id=after, device_id_type=MESH)
    backward = pltpu.make_async_remote_copy(
        src_ref=hs.at[BACK:7], dst_ref=hr.at[BACK:7], send_sem=hsem.at[1], recv_sem=hrsem.at[1],
        device_id=before, device_id_type=MESH)
    forward.start()
    backward.start()

    last = jnp.where(chan == 63, 0.0, 1.0).astype(F32)
    first = jnp.where(chan == 0, 0.0, 1.0).astype(F32)

    def fir(lo, hi, masked):
        @pl.loop(0, 32)
        def _(idx):
            nt = idx // 4
            row = lax.rem(idx, 4) * 16
            lanes = pl.ds(pl.multiple_of(nt * 128, 128), 128)
            taps = [proto[t:t + 1, lanes] for t in range(TAPS)]
            frames = {}
            for f in range(lo, hi + TAPS - 1):
                value = vt[nt, pl.ds(pl.multiple_of(f * INP + row, 16), 16), :]
                frames[f] = value * last if masked and f < BACK + SPEC else value
            for j in range(lo, hi):
                total = taps[0] * frames[j]
                for t in range(1, TAPS):
                    total = total + taps[t] * frames[j + t]
                filt[pl.ds(pl.multiple_of(j * INP + row, 16), 16), lanes] = total.astype(BF16)

    fir(BACK, SPEC - AHEAD, False)

    low = lax.broadcasted_iota(jnp.int32, (NM // 2, 128), 1) < 64

    def dft(ch, groups):
        lhs = jnp.concatenate(
            [table[lax.rem(z + s * ROLES[u] + NZ, NZ), (s + 1) // 2] for u in range(4 * ch, 4 * ch + 4) for s in (-1, 1)],
            axis=0)
        for sg in groups:
            full = lax.dot_general(lhs, filt[sg * 256:(sg + 1) * 256, :], (((1,), (1,)), ((), ())),
                                   preferred_element_type=F32)
            for uc in range(8):
                for s2 in range(2):
                    re = full[uc * 32:uc * 32 + 16, s2 * 128:(s2 + 1) * 128]
                    im = full[uc * 32 + 16:uc * 32 + 32, s2 * 128:(s2 + 1) * 128]
                    even = jnp.where(low, re, pltpu.roll(im, 64, 1))
                    odd = jnp.where(low, pltpu.roll(re, 64, 1), im)
                    row = ((uc // 2) * NM + uc % 2) * SPEC + sg * 4 + s2 * 2
                    stage[pl.ds(row, NM // 2, stride=2 * SPEC), :] = even
                    stage[pl.ds(row + 1, NM // 2, stride=2 * SPEC), :] = odd

    def send_plane(ch):
        @pl.loop(0, NM)
        def _(m):
            for u in range(4):
                start = pl.multiple_of((u * NM + m) * SPEC, SPEC)
                sendp[4 * ch + u, m] = stage[pl.ds(start, SPEC), :].astype(BF16)

        own = pltpu.make_async_copy(sendp.at[4 * ch:4 * ch + 4, mine], recvp.at[4 * ch:4 * ch + 4, mine], prsem.at[ch])
        own.start()

        @pl.loop(1, NM)
        def _(k):
            m = lax.rem(mine + k, NM)
            pltpu.make_async_remote_copy(
                src_ref=sendp.at[4 * ch:4 * ch + 4, m], dst_ref=recvp.at[4 * ch:4 * ch + 4, mine],
                send_sem=psem, recv_sem=prsem.at[ch], device_id=in_plane(m), device_id_type=MESH).start()

    def send_column(ch):
        block = recvp.at[4 * ch:4 * ch + 4]
        pltpu.make_async_copy(block, block, prsem.at[ch]).wait()
        for u in range(4 * ch, 4 * ch + 4):
            role = ROLES[u]
            hub = hub_of(role)
            if role == hub:
                continue
            side = 0 if hub > 0 else (1 if hub < 0 else 2)
            slot = (SIDE_A, SIDE_B, SIDE_C)[side].index(role)
            pltpu.make_async_remote_copy(
                src_ref=recvp.at[u], dst_ref=(za, zb, zc)[side].at[slot], send_sem=zsem, recv_sem=zrsem.at[side],
                device_id=in_column(sgn * (hub - role)), device_id_type=MESH).start()

    dft(0, (1, 2))
    forward.wait_recv()
    backward.wait_recv()

    @pl.loop(0, 8)
    def _(nt):
        for n, f in enumerate([0, 1, 2, 3, 20, 21, 22]):
            value = hr[n, nt].astype(F32)
            vt[nt, f * INP:(f + 1) * INP, :] = value * first if f < BACK else value

    fir(0, BACK, False)
    fir(SPEC - AHEAD, SPEC, True)
    dft(0, (0, 3))
    send_plane(0)
    dft(1, range(4))
    send_plane(1)
    send_column(0)
    dft(2, range(4))
    send_plane(2)
    send_column(1)
    dft(3, range(4))
    send_plane(3)
    send_column(2)
    send_column(3)

    flip = jnp.where(lax.broadcasted_iota(jnp.int32, (64, 128), 1) < 64, 1.0, -1.0).astype(F32)

    def group_rows(g, held, own):
        planes = held.shape[0]
        part = pl.ds(g * 4, 4)
        return jnp.concatenate(
            [held[:, part].reshape(planes * 64, 128), recvp[own, part].reshape(64, 128)], axis=0)

    def products(w, held, role, lags):
        own = ROLES.index(role)
        left = group_rows(lax.rem(grp + 1 + w, NG), held, own)
        right = [left] + [group_rows(lax.rem(grp + 1 + w - lag + NG, NG), held, own) for lag in range(1, lags)]
        full = lax.dot_general(left, jnp.concatenate(right, axis=1), (((0,), (0,)), ((), ())),
                               preferred_element_type=F32)
        blocks = []
        for lag in range(lags):
            part = full[:, lag * 128:(lag + 1) * 128]
            blocks.append(part[0:64] * flip + pltpu.roll(part[64:128], 64, 1))
        return blocks

    def partial(w, lags, held, role, sums, landing, side, offset):
        for lag, block in enumerate(products(w, held, role, lags)):
            sums[w, lag] = block.astype(BF16)
        pltpu.make_async_remote_copy(
            src_ref=sums.at[w, 0:lags], dst_ref=landing.at[w, 0:lags], send_sem=qsem, recv_sem=qrsem.at[side, w],
            device_id=in_column(offset), device_id_type=MESH).start()

    pltpu.make_async_copy(za, za, zrsem.at[0]).wait()
    pltpu.make_async_copy(zb, zb, zrsem.at[1]).wait()
    for base, lags in ((0, 5), (4, 4)):
        @pl.loop(base, base + 4)
        def _(w):
            partial(w, lags, za, HUB, pa, qa, 0, -sgn * HUB)
            partial(w, lags, zb, -HUB, pb, qb, 1, sgn * HUB)

    pltpu.make_async_copy(zc, zc, zrsem.at[2]).wait()
    scale = 1.0 / 32.0

    def reply(w):
        return pltpu.make_async_remote_copy(
            src_ref=fin.at[w], dst_ref=rr.at[w], send_sem=rsem, recv_sem=rrsem.at[w],
            device_id=(lax.rem(grp + 1 + w, NG), chan), device_id_type=MESH)

    def finish(w, lags):
        for side, landing in ((0, qa), (1, qb)):
            here = landing.at[w, 0:lags]
            pltpu.make_async_copy(here, here, qrsem.at[side, w]).wait()
        for lag, block in enumerate(products(w, zc, 0, lags)):
            fin[w, lag] = (block + qa[w, lag].astype(F32) + qb[w, lag].astype(F32)) * scale
        if lags < NL:
            other = fin[w - 4, 4]
            square = jnp.concatenate([other, pltpu.roll(other, 64, 1)], axis=0)
            fin[w, 4] = square.T[0:64] * flip

    @pl.loop(0, 4)
    def _(w):
        finish(w, 5)
        reply(w).start()

    @pl.loop(4, 7)
    def _(w):
        finish(w, 4)
        reply(w).start()

    finish(7, 4)

    def deliver(w, source):
        c8 = lax.rem(grp - 1 - w + 2 * NG, NG)
        for lag in range(NL):
            block = source[w, lag]
            out[0, lag, c8, 0] = block[:, 0:64]
            out[0, lag, c8, 1] = pltpu.roll(block, 64, 1)[:, 0:64]

    deliver(7, fin)

    @pl.loop(0, 7)
    def _(w):
        pltpu.make_async_copy(rr.at[w], rr.at[w], rrsem.at[w]).wait()
        deliver(w, rr)

    forward.wait_send()
    backward.wait_send()

    def drain(ref, sem):
        pltpu.make_async_copy(ref, ref, sem).wait()

    drain(sendp.at[:, 0:NM - 1], psem)
    drain(recvp.at[0:len(SIDE_A) + len(SIDE_B) + len(SIDE_C)], zsem)
    for sums in (pa, pb):
        drain(sums.at[0:4], qsem)
        drain(sums.at[4:8, 0:4], qsem)
    drain(fin.at[0:7], rsem)


def shards(voltages, prototype):
    call = pl.pallas_call(
        kernel,
        out_shape=jax.ShapeDtypeStruct((1, NL, NG, 2, 64, 64), F32),
        in_specs=[pl.BlockSpec(memory_space=pltpu.VMEM)] * 3,
        out_specs=pl.BlockSpec(memory_space=pltpu.VMEM),
        scratch_shapes=[
            pltpu.VMEM((8, 24 * INP, 128), F32),
            pltpu.VMEM((7, 8, INP, 128), BF16),
            pltpu.VMEM((7, 8, INP, 128), BF16),
            pltpu.VMEM((SPEC * INP, FRAME), BF16),
            pltpu.VMEM((4 * NM * SPEC, 128), F32),
            pltpu.VMEM((NZ, NM, SPEC, 128), BF16),
            pltpu.VMEM((NZ, NM, SPEC, 128), BF16),
            pltpu.VMEM((len(SIDE_A), NM, SPEC, 128), BF16),
            pltpu.VMEM((len(SIDE_B), NM, SPEC, 128), BF16),
            pltpu.VMEM((len(SIDE_C), NM, SPEC, 128), BF16),
            pltpu.VMEM((8, NL, 64, 128), BF16),
            pltpu.VMEM((8, NL, 64, 128), BF16),
            pltpu.VMEM((8, NL, 64, 128), BF16),
            pltpu.VMEM((8, NL, 64, 128), BF16),
            pltpu.VMEM((8, NL, 64, 128), F32),
            pltpu.VMEM((8, NL, 64, 128), F32),
            pltpu.SemaphoreType.DMA((2,)),
            pltpu.SemaphoreType.DMA((2,)),
            pltpu.SemaphoreType.DMA,
            pltpu.SemaphoreType.DMA((4,)),
            pltpu.SemaphoreType.DMA,
            pltpu.SemaphoreType.DMA((3,)),
            pltpu.SemaphoreType.DMA,
            pltpu.SemaphoreType.DMA((2, 8)),
            pltpu.SemaphoreType.DMA,
            pltpu.SemaphoreType.DMA((8,)),
        ],
        compiler_params=pltpu.CompilerParams(
            collective_id=0, has_side_effects=True, vmem_limit_bytes=56 << 20),
        cost_estimate=pl.CostEstimate(flops=4_000_000_000, bytes_accessed=8_000_000, transcendentals=0),
        name="fx",
    )
    return call(voltages, prototype, jnp.asarray(dft_table()))


def solution(mesh):
    in_specs = (P("grp", "chan", None), P())
    out_specs = P("grp", None, "chan", None, None, None)
    return jax.shard_map(shards, mesh=mesh, in_specs=in_specs, out_specs=out_specs, check_vma=False)
```

time: 390 us -> 131 us (0.34)
  the two profiles are of different devices: /device:TPU:32 before, /device:TPU:1 now
where the time goes in v1:
time: 131 us
  Pallas kernels  127 us (97%)
  local copies, waits for them, and re-layouts  3.56 us (3%)
    pallas_call x1, Pallas kernels, shards(): return call(voltages, prototype, jnp.asarray(dft_table()))  127 us
    unnamed x1, local copies, waits for them, and re-layouts  3.56 us

profile of v1, /device:TPU:1, one launch (start us, length us, event | category | flops | bytes accessed | tf_op | source)
XLA Modules:
  0.0 130.9 jit_solution(2858917665079323452)
XLA Ops:
  0.0 127.3 %fx.1 = f32[1,5,8,2,64,64]{5,4,3,2,1,0:T(8,128)} custom-call(bf16[64,16,1024]{2,1,0:T(8,128)(2,1)} %volt.1, f32[8,1024]{1,0:T(8,128)} %proto.1, bf16[16,2,32,1024]{3,2,1,0:T(8,128)(2,1)} %constant.2.clone.table), custom_call_target="tpu_custom_call" | custom-call | flops 4000000000 | bytes 8000000 | tf_op jit(solution)/shard_map/fx/pallas_call | solution.py:323
  127.3 3.6 %copy.5 = f32[1,5,8,2,64,64]{5,4,3,2,1,0:T(8,128)} copy(f32[1,5,8,2,64,64]{5,4,3,2,1,0:T(8,128)} %fx.1) | data formatting | bytes 2621440

commit v2 on v1

v2 whole, which is shorter than its diff:
```python
import math

import jax
import jax.numpy as jnp
import numpy as np
from jax import lax
from jax.experimental import pallas as pl
from jax.experimental.pallas import tpu as pltpu
from jax.sharding import PartitionSpec as P

MESH = pl.DeviceIdType.MESH
BF16, F32 = jnp.bfloat16, jnp.float32

TAPS, FRAME, INP, SPEC = 8, 1024, 64, 16
NZ, NM, NG, NL = 16, 32, 8, 5
BACK, AHEAD = 4, 3
ROLES = [7, -7, 8] + [s * r for r in range(6, 0, -1) for s in (1, -1)] + [0]
HUB = 3
DIRECT = 2
CHUNKS = ((2, 4), (4, 8), (8, 12), (12, 16))


def hub_of(role):
    return 0 if abs(role) < 2 else (HUB if role > 0 else -HUB)


SIDE_A = [r for r in ROLES if hub_of(r) == HUB and r != HUB]
SIDE_B = [r for r in ROLES if hub_of(r) == -HUB and r != -HUB]
SIDE_C = [r for r in ROLES if hub_of(r) == 0 and r != 0]


def dft_table():
    m = np.arange(NM)
    plane = np.arange(NZ)[:, None]
    chan = (((m // 2) % 2) * NZ + plane) * 2 + m % 2
    k = 8 * chan + m // 4
    phase = (k[:, :, None] * np.arange(FRAME)) % FRAME * (2.0 * np.pi / FRAME)
    table = np.stack([np.cos(phase), -np.sin(phase)], axis=1) / math.sqrt(FRAME)
    table = table.reshape(NZ, 2, NM // 2, 2, FRAME).transpose(0, 3, 1, 2, 4)
    return table.reshape(NZ, 2, NM, FRAME).astype(jnp.bfloat16)


def kernel(volt_hbm, proto, table_hbm, out, volt, table, vt, hs, hr, filt, stage, sendp, recvp, za, zb, zc,
           pa, pb, qa, qb, fin, plane_in, insem, hsem, hrsem, psem, prsem, zsem, zrsem, qsem, qrsem, rsem, rrsem):
    grp = lax.axis_index("grp")
    chan = lax.axis_index("chan")
    core = lax.rem(chan, 2)
    z = lax.rem(chan // 2, NZ)
    ylo = chan // (2 * NZ)
    mine = grp * 4 + ylo * 2 + core
    sgn = 1 - 2 * core

    def in_plane(m, offset=0):
        return (m // 4, (lax.rem(m // 2, 2) * NZ + lax.rem(z + offset + NZ, NZ)) * 2 + lax.rem(m, 2))

    def in_column(offset):
        return (grp, (ylo * NZ + lax.rem(z + offset + 2 * NZ, NZ)) * 2 + core)

    after = (grp, lax.rem(chan + 1, 64))
    before = (grp, lax.rem(chan + 63, 64))
    beyond = (grp, lax.rem(chan + 63 + 2 * core, 64))

    fetches = [
        pltpu.make_async_copy(volt_hbm.at[n * 16:(n + 1) * 16], volt.at[n * 16:(n + 1) * 16], insem.at[n])
        for n in range(4)
    ]
    fetch_table = pltpu.make_async_copy(table_hbm, table, insem.at[4])
    for fetch in fetches:
        fetch.start()
    barrier = pltpu.get_barrier_semaphore()

    @pl.loop(1, NM)
    def _(k):
        pl.semaphore_signal(barrier, inc=1, device_id=in_plane(lax.rem(mine + k, NM)), device_id_type=MESH)

    for d in (1, 2, 3, 4, 5):
        for s in (1, -1):
            pl.semaphore_signal(barrier, inc=1, device_id=in_column(s * d), device_id_type=MESH)
    pl.semaphore_signal(barrier, inc=1, device_id=beyond, device_id_type=MESH)

    for n in range(4):
        fetches[n].wait()
        if n == 3:
            fetch_table.start()

        @pl.loop(n * 16, (n + 1) * 16)
        def _(i):
            for nt in range(8):
                tile = volt[i, :, nt * 128:(nt + 1) * 128].astype(F32)
                vt[nt, pl.ds(BACK * INP + i, SPEC, stride=INP), :] = tile

    @pl.loop(0, 8)
    def _(nt):
        for n, f in enumerate([16, 17, 18, 19, 4, 5, 6]):
            hs[n, nt] = vt[nt, f * INP:(f + 1) * INP, :].astype(BF16)

    pl.semaphore_wait(barrier, NM - 1 + 11)
    for offset in (HUB - 7, 7 - HUB):
        pl.semaphore_signal(plane_in, inc=1, device_id=in_column(offset), device_id_type=MESH)
    forward = pltpu.make_async_remote_copy(
        src_ref=hs.at[0:BACK], dst_ref=hr.at[0:BACK], send_sem=hsem.at[0], recv_sem=hrsem.at[0],
        device_id=after, device_id_type=MESH)
    backward = pltpu.make_async_remote_copy(
        src_ref=hs.at[BACK:7], dst_ref=hr.at[BACK:7], send_sem=hsem.at[1], recv_sem=hrsem.at[1],
        device_id=before, device_id_type=MESH)
    forward.start()
    backward.start()

    last = jnp.where(chan == 63, 0.0, 1.0).astype(F32)
    first = jnp.where(chan == 0, 0.0, 1.0).astype(F32)

    def fir(lo, hi, masked):
        @pl.loop(0, 32)
        def _(idx):
            nt = idx // 4
            row = lax.rem(idx, 4) * 16
            lanes = pl.ds(pl.multiple_of(nt * 128, 128), 128)
            taps = [proto[t:t + 1, lanes] for t in range(TAPS)]
            frames = {}
            for f in range(lo, hi + TAPS - 1):
                value = vt[nt, pl.ds(pl.multiple_of(f * INP + row, 16), 16), :]
                frames[f] = value * last if masked and f < BACK + SPEC else value
            for j in range(lo, hi):
                total = taps[0] * frames[j]
                for t in range(1, TAPS):
                    total = total + taps[t] * frames[j + t]
                filt[pl.ds(pl.multiple_of(j * INP + row, 16), 16), lanes] = total.astype(BF16)

    fir(BACK, SPEC - AHEAD, False)

    low = lax.broadcasted_iota(jnp.int32, (NM // 2, 128), 1) < 64

    def dft(first_u, last_u, groups):
        lhs = jnp.concatenate(
            [table[lax.rem(z + s * ROLES[u] + NZ, NZ), (s + 1) // 2] for u in range(first_u, last_u) for s in (-1, 1)],
            axis=0)
        for sg in groups:
            full = lax.dot_general(lhs, filt[sg * 256:(sg + 1) * 256, :], (((1,), (1,)), ((), ())),
                                   preferred_element_type=F32)
            for uc in range(2 * (last_u - first_u)):
                for s2 in range(2):
                    re = full[uc * 32:uc * 32 + 16, s2 * 128:(s2 + 1) * 128]
                    im = full[uc * 32 + 16:uc * 32 + 32, s2 * 128:(s2 + 1) * 128]
                    even = jnp.where(low, re, pltpu.roll(im, 64, 1))
                    odd = jnp.where(low, pltpu.roll(re, 64, 1), im)
                    row = ((first_u + uc // 2) * NM + uc % 2) * SPEC + sg * 4 + s2 * 2
                    stage[pl.ds(row, NM // 2, stride=2 * SPEC), :] = even
                    stage[pl.ds(row + 1, NM // 2, stride=2 * SPEC), :] = odd

    def pack(lo, hi):
        @pl.loop(0, NM)
        def _(m):
            for u in range(lo, hi):
                start = pl.multiple_of((u * NM + m) * SPEC, SPEC)
                sendp[u, m] = stage[pl.ds(start, SPEC), :].astype(BF16)

    def send_direct():
        pack(0, DIRECT)
        pl.semaphore_wait(plane_in, 2)

        @pl.loop(0, NM)
        def _(k):
            m = lax.rem(mine + k, NM)
            for u in range(DIRECT):
                side = 0 if ROLES[u] > 0 else 1
                slot = (SIDE_A, SIDE_B)[side].index(ROLES[u])
                offset = (1 - 2 * lax.rem(m, 2)) * (hub_of(ROLES[u]) - ROLES[u])
                pltpu.make_async_remote_copy(
                    src_ref=sendp.at[u, m], dst_ref=(za, zb)[side].at[slot, mine], send_sem=zsem,
                    recv_sem=zrsem.at[side], device_id=in_plane(m, offset), device_id_type=MESH).start()

    def send_plane(ch):
        lo, hi = CHUNKS[ch]
        pack(lo, hi)
        pltpu.make_async_copy(sendp.at[lo:hi, mine], recvp.at[lo:hi, mine], prsem.at[ch]).start()

        @pl.loop(1, NM)
        def _(k):
            m = lax.rem(mine + k, NM)
            pltpu.make_async_remote_copy(
                src_ref=sendp.at[lo:hi, m], dst_ref=recvp.at[lo:hi, mine],
                send_sem=psem, recv_sem=prsem.at[ch], device_id=in_plane(m), device_id_type=MESH).start()

    def send_column(ch):
        lo, hi = CHUNKS[ch]
        block = recvp.at[lo:hi]
        pltpu.make_async_copy(block, block, prsem.at[ch]).wait()
        for u in range(lo, hi):
            role = ROLES[u]
            hub = hub_of(role)
            if role == hub:
                continue
            side = 0 if hub > 0 else (1 if hub < 0 else 2)
            slot = (SIDE_A, SIDE_B, SIDE_C)[side].index(role)
            pltpu.make_async_remote_copy(
                src_ref=recvp.at[u], dst_ref=(za, zb, zc)[side].at[slot], send_sem=zsem, recv_sem=zrsem.at[side],
                device_id=in_column(sgn * (hub - role)), device_id_type=MESH).start()

    fetch_table.wait()
    for u in range(0, NZ, 4):
        dft(u, u + 4, (1, 2))
    forward.wait_recv()
    backward.wait_recv()

    @pl.loop(0, 8)
    def _(nt):
        for n, f in enumerate([0, 1, 2, 3, 20, 21, 22]):
            value = hr[n, nt].astype(F32)
            vt[nt, f * INP:(f + 1) * INP, :] = value * first if f < BACK else value

    fir(0, BACK, False)
    fir(SPEC - AHEAD, SPEC, True)
    dft(0, DIRECT, (0, 3))
    send_direct()
    for ch, (lo, hi) in enumerate(CHUNKS):
        dft(lo, hi, (0, 3))
        send_plane(ch)
        if ch:
            send_column(ch - 1)
    send_column(len(CHUNKS) - 1)

    flip = jnp.where(lax.broadcasted_iota(jnp.int32, (64, 128), 1) < 64, 1.0, -1.0).astype(F32)

    def group_rows(g, held, own):
        planes = held.shape[0]
        part = pl.ds(g * 4, 4)
        return jnp.concatenate(
            [held[:, part].reshape(planes * 64, 128), recvp[own, part].reshape(64, 128)], axis=0)

    def products(w, held, role, lags):
        own = ROLES.index(role)
        left = group_rows(lax.rem(grp + 1 + w, NG), held, own)
        right = [left] + [group_rows(lax.rem(grp + 1 + w - lag + NG, NG), held, own) for lag in range(1, lags)]
        full = lax.dot_general(left, jnp.concatenate(right, axis=1), (((0,), (0,)), ((), ())),
                               preferred_element_type=F32)
        blocks = []
        for lag in range(lags):
            part = full[:, lag * 128:(lag + 1) * 128]
            blocks.append(part[0:64] * flip + pltpu.roll(part[64:128], 64, 1))
        return blocks

    row = lax.broadcasted_iota(jnp.int32, (64, 128), 0)
    lane = lax.broadcasted_iota(jnp.int32, (64, 128), 1)
    left_half = lane < 64
    column = jnp.where(left_half, lane, lane - 64)

    def folded(one, two):
        lower = row >= column
        return jnp.where(left_half, jnp.where(lower, one, pltpu.roll(one, 64, 1)),
                         jnp.where(lower, pltpu.roll(two, 64, 1), two))

    def unfolded(value):
        both = jnp.where(left_half, value, pltpu.roll(value, 64, 1))
        turned = jnp.concatenate([value, value], axis=0).T[0:64]
        real = jnp.where(row >= column, both, turned)
        imag = jnp.where(row < column, both, jnp.where(row > column, -turned, 0.0))
        return jnp.where(left_half, real, imag)

    def partial(pair, lags, held, role, sums, landing, side, offset):
        diagonal = []
        for half in range(2):
            blocks = products(pair + half, held, role, lags)
            diagonal.append(blocks[0])
            for lag in range(1, lags):
                sums[pair + half, lag - 1] = blocks[lag].astype(BF16)
        sums[pair, lags - 1] = folded(*diagonal).astype(BF16)
        for half in range(2):
            w = pair + half
            pltpu.make_async_remote_copy(
                src_ref=sums.at[w, 0:lags - half], dst_ref=landing.at[w, 0:lags - half], send_sem=qsem,
                recv_sem=qrsem.at[side, w], device_id=in_column(offset), device_id_type=MESH).start()

    pltpu.make_async_copy(za, za, zrsem.at[0]).wait()
    pltpu.make_async_copy(zb, zb, zrsem.at[1]).wait()
    for base, lags in ((0, 5), (4, 4)):
        @pl.loop(0, 2)
        def _(p):
            partial(base + 2 * p, lags, za, HUB, pa, qa, 0, -sgn * HUB)
            partial(base + 2 * p, lags, zb, -HUB, pb, qb, 1, sgn * HUB)

    pltpu.make_async_copy(zc, zc, zrsem.at[2]).wait()
    for base, lags in ((0, 5), (4, 4)):
        @pl.loop(base, base + 4)
        def _(w):
            for lag, block in enumerate(products(w, zc, 0, lags)):
                fin[w, lag] = block

    scale = 1.0 / 32.0

    def reply(w):
        pltpu.make_async_remote_copy(
            src_ref=fin.at[w], dst_ref=out.at[grp], send_sem=rsem, recv_sem=rrsem.at[w],
            device_id=(lax.rem(grp + 1 + w, NG), chan), device_id_type=MESH).start()

    def finish(pair, lags):
        for half in range(2):
            w = pair + half
            for side, landing in ((0, qa), (1, qb)):
                here = landing.at[w, 0:lags - half]
                pltpu.make_async_copy(here, here, qrsem.at[side, w]).wait()
            for lag in range(1, lags):
                fin[w, lag] = (fin[w, lag] + qa[w, lag - 1].astype(F32) + qb[w, lag - 1].astype(F32)) * scale
            if lags == NL:
                other = fin[w, 4]
                square = jnp.concatenate([other, pltpu.roll(other, 64, 1)], axis=0)
                fin[w + 4, 4] = square.T[0:64] * flip
            if not half:
                packed = qa[w, lags - 1].astype(F32) + qb[w, lags - 1].astype(F32)
                fin[w, 0] = (fin[w, 0] + unfolded(packed)) * scale
                fin[w + 1, 0] = (fin[w + 1, 0] + unfolded(pltpu.roll(packed, 64, 1))) * scale
            if not (isinstance(w, int) and w == 7):
                reply(w)

    @pl.loop(0, 2)
    def _(p):
        finish(2 * p, 5)

    finish(4, 4)
    finish(6, 4)
    keep = pltpu.make_async_copy(fin.at[7], out.at[grp], insem.at[0])
    keep.start()
    for w in range(7):
        here = out.at[lax.rem(grp - 1 - w + 2 * NG, NG)]
        pltpu.make_async_copy(here, here, rrsem.at[w]).wait()
    keep.wait()

    forward.wait_send()
    backward.wait_send()

    def drain(ref, sem):
        pltpu.make_async_copy(ref, ref, sem).wait()

    drain(sendp.at[DIRECT:, 0:NM - 1], psem)
    drain(recvp.at[0:len(SIDE_A) + len(SIDE_B) + len(SIDE_C)], zsem)
    for sums in (pa, pb):
        drain(sums.at[0:8, 0:4], qsem)
    drain(fin.at[0:7], rsem)


def split(packed, out, held, parts, insem, outsem):
    def fetch(n):
        return pltpu.make_async_copy(packed.at[n], held.at[n], insem.at[n])

    for n in range(NG):
        fetch(n).start()
    for n in range(NG):
        fetch(n).wait()
        value = held[n]
        parts[:, n, 0] = value[:, :, 0:64]
        parts[:, n, 1] = pltpu.roll(value, 64, 2)[:, :, 0:64]
        pltpu.make_async_copy(parts.at[:, n], out.at[0, :, n], outsem).start()
    pltpu.make_async_copy(parts, out.at[0], outsem).wait()


def shards(voltages, prototype):
    anywhere = pl.BlockSpec(memory_space=pl.ANY)
    call = pl.pallas_call(
        kernel,
        out_shape=jax.ShapeDtypeStruct((NG, NL, 64, 128), F32),
        in_specs=[anywhere, pl.BlockSpec(memory_space=pltpu.VMEM), anywhere],
        out_specs=anywhere,
        scratch_shapes=[
            pltpu.VMEM((INP, SPEC, FRAME), BF16),
            pltpu.VMEM((NZ, 2, NM, FRAME), BF16),
            pltpu.VMEM((8, 24 * INP, 128), F32),
            pltpu.VMEM((7, 8, INP, 128), BF16),
            pltpu.VMEM((7, 8, INP, 128), BF16),
            pltpu.VMEM((SPEC * INP, FRAME), BF16),
            pltpu.VMEM((NZ * NM * SPEC, 128), F32),
            pltpu.VMEM((NZ, NM, SPEC, 128), BF16),
            pltpu.VMEM((NZ, NM, SPEC, 128), BF16),
            pltpu.VMEM((len(SIDE_A), NM, SPEC, 128), BF16),
            pltpu.VMEM((len(SIDE_B), NM, SPEC, 128), BF16),
            pltpu.VMEM((len(SIDE_C), NM, SPEC, 128), BF16),
            pltpu.VMEM((8, NL, 64, 128), BF16),
            pltpu.VMEM((8, NL, 64, 128), BF16),
            pltpu.VMEM((8, NL, 64, 128), BF16),
            pltpu.VMEM((8, NL, 64, 128), BF16),
            pltpu.VMEM((8, NL, 64, 128), F32),
            pltpu.SemaphoreType.REGULAR,
            pltpu.SemaphoreType.DMA((5,)),
            pltpu.SemaphoreType.DMA((2,)),
            pltpu.SemaphoreType.DMA((2,)),
            pltpu.SemaphoreType.DMA,
            pltpu.SemaphoreType.DMA((len(CHUNKS),)),
            pltpu.SemaphoreType.DMA,
            pltpu.SemaphoreType.DMA((3,)),
            pltpu.SemaphoreType.DMA,
            pltpu.SemaphoreType.DMA((2, 8)),
            pltpu.SemaphoreType.DMA,
            pltpu.SemaphoreType.DMA((7,)),
        ],
        compiler_params=pltpu.CompilerParams(
            collective_id=0, has_side_effects=True, vmem_limit_bytes=56 << 20),
        cost_estimate=pl.CostEstimate(flops=4_000_000_000, bytes_accessed=8_000_000, transcendentals=0),
        name="fx",
    )
    packed = call(voltages, prototype, jnp.asarray(dft_table()))
    return pl.pallas_call(
        split,
        out_shape=jax.ShapeDtypeStruct((1, NL, NG, 2, 64, 64), F32),
        in_specs=[anywhere],
        out_specs=anywhere,
        scratch_shapes=[
            pltpu.VMEM((NG, NL, 64, 128), F32),
            pltpu.VMEM((NL, NG, 2, 64, 64), F32),
            pltpu.SemaphoreType.DMA((NG,)),
            pltpu.SemaphoreType.DMA,
        ],
        cost_estimate=pl.CostEstimate(flops=0, bytes_accessed=4_000_000, transcendentals=0),
        name="split",
    )(packed)


def solution(mesh):
    in_specs = (P("grp", "chan", None), P())
    out_specs = P("grp", None, "chan", None, None, None)
    return jax.shard_map(shards, mesh=mesh, in_specs=in_specs, out_specs=out_specs, check_vma=False)
```

time: 131 us -> 118 us (0.901)
  the two profiles are of different devices: /device:TPU:1 before, /device:TPU:16 now
where the time goes in v2:
time: 118 us
  Pallas kernels  118 us (100%)
    pallas_call x1, Pallas kernels, shards(): packed = call(voltages, prototype, jnp.asarray(dft_table()))  115 us
    pallas_call x1, Pallas kernels, shards(): pl.pallas_call(split, out_shape=jax.ShapeDtypeStruct((1, NL, NG, 2, 64, 6...  2.6 us

profile of v2, /device:TPU:16, one launch (start us, length us, event | category | flops | bytes accessed | tf_op | source)
XLA Modules:
  0.0 117.8 jit_solution(6215580022482185911)
XLA Ops:
  0.0 115.2 %fx.1.packed = f32[8,5,64,128]{3,2,1,0:T(8,128)} custom-call(bf16[64,16,1024]{2,1,0:T(8,128)(2,1)} %volt_hbm.1, f32[8,1024]{1,0:T(8,128)} %proto.1, bf16[16,2,32,1024]{3,2,1,0:T(8,128)(2,1)} %constant.2.clone.table_hbm), custom_call_target="tpu_custom_call" | custom-call | flops 4000000000 | bytes 8000000 | tf_op jit(solution)/shard_map/fx/pallas_call | solution.py:398
  115.2 2.6 %split.1 = f32[1,5,8,2,64,64]{5,4,3,2,1,0:T(8,128)} custom-call(f32[8,5,64,128]{3,2,1,0:T(8,128)} %fx.1.packed), custom_call_target="tpu_custom_call" | custom-call | bytes 4000000 | tf_op jit(solution)/shard_map/split/pallas_call | solution.py:399

commit v3 on v2

--- a/solution.py
+++ b/solution.py
@@ -40,7 +40,7 @@
     return table.reshape(NZ, 2, NM, FRAME).astype(jnp.bfloat16)
 
 
-def kernel(volt_hbm, proto, table_hbm, out, volt, table, vt, hs, hr, filt, stage, sendp, recvp, za, zb, zc,
+def kernel(volt_hbm, proto, table_hbm, out, volt, table, vt, begun, hs, hr, filt, stage, sendp, recvp, za, zb, zc,
            pa, pb, qa, qb, fin, plane_in, insem, hsem, hrsem, psem, prsem, zsem, zrsem, qsem, qrsem, rsem, rrsem):
     grp = lax.axis_index("grp")
     chan = lax.axis_index("chan")
@@ -87,11 +87,11 @@
         def _(i):
             for nt in range(8):
                 tile = volt[i, :, nt * 128:(nt + 1) * 128].astype(F32)
-                vt[nt, pl.ds(BACK * INP + i, SPEC, stride=INP), :] = tile
+                vt[nt, pl.ds(i, SPEC, stride=INP), :] = tile
 
     @pl.loop(0, 8)
     def _(nt):
-        for n, f in enumerate([16, 17, 18, 19, 4, 5, 6]):
+        for n, f in enumerate([12, 13, 14, 15, 0, 1, 2]):
             hs[n, nt] = vt[nt, f * INP:(f + 1) * INP, :].astype(BF16)
 
     pl.semaphore_wait(barrier, NM - 1 + 11)
@@ -109,24 +109,45 @@
     last = jnp.where(chan == 63, 0.0, 1.0).astype(F32)
     first = jnp.where(chan == 0, 0.0, 1.0).astype(F32)
 
-    def fir(lo, hi, masked):
+    def over_tiles(body):
         @pl.loop(0, 32)
         def _(idx):
             nt = idx // 4
-            row = lax.rem(idx, 4) * 16
+            row = pl.multiple_of(lax.rem(idx, 4) * 16, 16)
             lanes = pl.ds(pl.multiple_of(nt * 128, 128), 128)
-            taps = [proto[t:t + 1, lanes] for t in range(TAPS)]
-            frames = {}
-            for f in range(lo, hi + TAPS - 1):
-                value = vt[nt, pl.ds(pl.multiple_of(f * INP + row, 16), 16), :]
-                frames[f] = value * last if masked and f < BACK + SPEC else value
-            for j in range(lo, hi):
-                total = taps[0] * frames[j]
-                for t in range(1, TAPS):
-                    total = total + taps[t] * frames[j + t]
-                filt[pl.ds(pl.multiple_of(j * INP + row, 16), 16), lanes] = total.astype(BF16)
-
-    fir(BACK, SPEC - AHEAD, False)
+            body(nt, row, lanes, [proto[t:t + 1, lanes] for t in range(TAPS)])
+
+    def own_frames(nt, row, lo, hi):
+        return {f: vt[nt, pl.ds(pl.multiple_of((f - BACK) * INP + row, 16), 16), :] for f in range(lo, hi)}
+
+    def summed(taps, frames, j):
+        terms = [taps[f - j] * frames[f] for f in range(j, j + TAPS) if f in frames]
+        return sum(terms[1:], terms[0])
+
+    edge = list(range(BACK)) + list(range(SPEC - AHEAD, SPEC))
+
+    def inner(nt, row, lanes, taps):
+        frames = own_frames(nt, row, BACK, BACK + SPEC)
+        for j in range(BACK, SPEC - AHEAD):
+            filt[pl.ds(pl.multiple_of(j * INP + row, 16), 16), lanes] = summed(taps, frames, j).astype(BF16)
+
+    def edge_begun(nt, row, lanes, taps):
+        frames = own_frames(nt, row, BACK, BACK + SPEC)
+        for n, j in enumerate(edge):
+            total = summed(taps, frames, j)
+            begun[n, nt, pl.ds(row, 16), :] = total if j < BACK else total * last
+
+    def edge_ended(nt, row, lanes, taps):
+        frames = {}
+        for n, f in enumerate([0, 1, 2, 3, 20, 21, 22]):
+            value = hr[n, nt, pl.ds(row, 16), :].astype(F32)
+            frames[f] = value * first if f < BACK else value
+        for n, j in enumerate(edge):
+            total = begun[n, nt, pl.ds(row, 16), :] + summed(taps, frames, j)
+            filt[pl.ds(pl.multiple_of(j * INP + row, 16), 16), lanes] = total.astype(BF16)
+
+    over_tiles(inner)
+    over_tiles(edge_begun)
 
     low = lax.broadcasted_iota(jnp.int32, (NM // 2, 128), 1) < 64
 
@@ -202,14 +223,7 @@
     forward.wait_recv()
     backward.wait_recv()
 
-    @pl.loop(0, 8)
-    def _(nt):
-        for n, f in enumerate([0, 1, 2, 3, 20, 21, 22]):
-            value = hr[n, nt].astype(F32)
-            vt[nt, f * INP:(f + 1) * INP, :] = value * first if f < BACK else value
-
-    fir(0, BACK, False)
-    fir(SPEC - AHEAD, SPEC, True)
+    over_tiles(edge_ended)
     dft(0, DIRECT, (0, 3))
     send_direct()
     for ch, (lo, hi) in enumerate(CHUNKS):
@@ -256,28 +270,61 @@
         imag = jnp.where(row < column, both, jnp.where(row > column, -turned, 0.0))
         return jnp.where(left_half, real, imag)
 
-    def partial(pair, lags, held, role, sums, landing, side, offset):
-        diagonal = []
-        for half in range(2):
-            blocks = products(pair + half, held, role, lags)
-            diagonal.append(blocks[0])
-            for lag in range(1, lags):
-                sums[pair + half, lag - 1] = blocks[lag].astype(BF16)
-        sums[pair, lags - 1] = folded(*diagonal).astype(BF16)
-        for half in range(2):
-            w = pair + half
+    sides = ((za, HUB, pa, qa, -sgn * HUB), (zb, -HUB, pb, qb, sgn * HUB))
+
+    def lags_of(w):
+        return 5 if w < 4 else 4
+
+    def form(pair):
+        lags = lags_of(pair)
+        for held, role, sums, _, _ in sides:
+            diagonal = []
+            for half in range(2):
+                blocks = products(pair + half, held, role, lags)
+                diagonal.append(blocks[0])
+                for lag in range(1, lags):
+                    sums[pair + half, lag - 1] = blocks[lag].astype(BF16)
+            sums[pair, lags - 1] = folded(*diagonal).astype(BF16)
+
+    def send(w):
+        count = lags_of(w) - w % 2
+        for side, (_, _, sums, landing, offset) in enumerate(sides):
             pltpu.make_async_remote_copy(
-                src_ref=sums.at[w, 0:lags - half], dst_ref=landing.at[w, 0:lags - half], send_sem=qsem,
+                src_ref=sums.at[w, 0:count], dst_ref=landing.at[w, 0:count], send_sem=qsem,
                 recv_sem=qrsem.at[side, w], device_id=in_column(offset), device_id_type=MESH).start()
+
+    scale = 1.0 / 32.0
+
+    def reply(w):
+        pltpu.make_async_remote_copy(
+            src_ref=fin.at[w], dst_ref=out.at[grp], send_sem=rsem, recv_sem=rrsem.at[w],
+            device_id=(lax.rem(grp + 1 + w, NG), chan), device_id_type=MESH).start()
+
+    def finish(w):
+        lags = lags_of(w)
+        for side, landing in ((0, qa), (1, qb)):
+            here = landing.at[w, 0:lags - w % 2]
+            pltpu.make_async_copy(here, here, qrsem.at[side, w]).wait()
+        for lag in range(1, lags):
+            fin[w, lag] = (fin[w, lag] + qa[w, lag - 1].astype(F32) + qb[w, lag - 1].astype(F32)) * scale
+        if lags == NL:
+            other = fin[w, 4]
+            square = jnp.concatenate([other, pltpu.roll(other, 64, 1)], axis=0)
+            fin[w + 4, 4] = square.T[0:64] * flip
+        if w % 2 == 0:
+            packed = qa[w, lags - 1].astype(F32) + qb[w, lags - 1].astype(F32)
+            fin[w, 0] = (fin[w, 0] + unfolded(packed)) * scale
+            fin[w + 1, 0] = (fin[w + 1, 0] + unfolded(pltpu.roll(packed, 64, 1))) * scale
+        if w < 7:
+            reply(w)
 
     pltpu.make_async_copy(za, za, zrsem.at[0]).wait()
     pltpu.make_async_copy(zb, zb, zrsem.at[1]).wait()
-    for base, lags in ((0, 5), (4, 4)):
-        @pl.loop(0, 2)
-        def _(p):
-            partial(base + 2 * p, lags, za, HUB, pa, qa, 0, -sgn * HUB)
-            partial(base + 2 * p, lags, zb, -HUB, pb, qb, 1, sgn * HUB)
-
+    form(0)
+    send(0)
+    send(1)
+    form(2)
+    send(2)
     pltpu.make_async_copy(zc, zc, zrsem.at[2]).wait()
     for base, lags in ((0, 5), (4, 4)):
         @pl.loop(base, base + 4)
@@ -285,38 +332,12 @@
             for lag, block in enumerate(products(w, zc, 0, lags)):
                 fin[w, lag] = block
 
-    scale = 1.0 / 32.0
-
-    def reply(w):
-        pltpu.make_async_remote_copy(
-            src_ref=fin.at[w], dst_ref=out.at[grp], send_sem=rsem, recv_sem=rrsem.at[w],
-            device_id=(lax.rem(grp + 1 + w, NG), chan), device_id_type=MESH).start()
-
-    def finish(pair, lags):
-        for half in range(2):
-            w = pair + half
-            for side, landing in ((0, qa), (1, qb)):
-                here = landing.at[w, 0:lags - half]
-                pltpu.make_async_copy(here, here, qrsem.at[side, w]).wait()
-            for lag in range(1, lags):
-                fin[w, lag] = (fin[w, lag] + qa[w, lag - 1].astype(F32) + qb[w, lag - 1].astype(F32)) * scale
-            if lags == NL:
-                other = fin[w, 4]
-                square = jnp.concatenate([other, pltpu.roll(other, 64, 1)], axis=0)
-                fin[w + 4, 4] = square.T[0:64] * flip
-            if not half:
-                packed = qa[w, lags - 1].astype(F32) + qb[w, lags - 1].astype(F32)
-                fin[w, 0] = (fin[w, 0] + unfolded(packed)) * scale
-                fin[w + 1, 0] = (fin[w + 1, 0] + unfolded(pltpu.roll(packed, 64, 1))) * scale
-            if not (isinstance(w, int) and w == 7):
-                reply(w)
-
-    @pl.loop(0, 2)
-    def _(p):
-        finish(2 * p, 5)
-
-    finish(4, 4)
-    finish(6, 4)
+    for w in range(8):
+        finish(w)
+        if w < 5:
+            if w % 2:
+                form(w + 3)
+            send(w + 3)
     keep = pltpu.make_async_copy(fin.at[7], out.at[grp], insem.at[0])
     keep.start()
     for w in range(7):
@@ -362,7 +383,8 @@
         scratch_shapes=[
             pltpu.VMEM((INP, SPEC, FRAME), BF16),
             pltpu.VMEM((NZ, 2, NM, FRAME), BF16),
-            pltpu.VMEM((8, 24 * INP, 128), F32),
+            pltpu.VMEM((8, SPEC * INP, 128), F32),
+            pltpu.VMEM((7, 8, INP, 128), F32),
             pltpu.VMEM((7, 8, INP, 128), BF16),
             pltpu.VMEM((7, 8, INP, 128), BF16),
             pltpu.VMEM((SPEC * INP, FRAME), BF16),

time: 118 us -> 117 us (level)
  the two profiles are of different devices: /device:TPU:16 before, /device:TPU:52 now
where the time goes in v3:
time: 117 us
  Pallas kernels  117 us (100%)
    pallas_call x1, Pallas kernels, shards(): packed = call(voltages, prototype, jnp.asarray(dft_table()))  114 us
    pallas_call x1, Pallas kernels, shards(): pl.pallas_call(split, out_shape=jax.ShapeDtypeStruct((1, NL, NG, 2, 64, 6...  2.6 us

profile of v3, /device:TPU:52, one launch (start us, length us, event | category | flops | bytes accessed | tf_op | source)
XLA Modules:
  0.0 117.0 jit_solution(16412296205023203477)
XLA Ops:
  0.0 114.4 %fx.1.packed = f32[8,5,64,128]{3,2,1,0:T(8,128)} custom-call(bf16[64,16,1024]{2,1,0:T(8,128)(2,1)} %volt_hbm.1, f32[8,1024]{1,0:T(8,128)} %proto.1, bf16[16,2,32,1024]{3,2,1,0:T(8,128)(2,1)} %constant.2.clone.table_hbm), custom_call_target="tpu_custom_call" | custom-call | flops 4000000000 | bytes 8000000 | tf_op jit(solution)/shard_map/fx/pallas_call | solution.py:420
  114.4 2.6 %split.1 = f32[1,5,8,2,64,64]{5,4,3,2,1,0:T(8,128)} custom-call(f32[8,5,64,128]{3,2,1,0:T(8,128)} %fx.1.packed), custom_call_target="tpu_custom_call" | custom-call | bytes 4000000 | tf_op jit(solution)/shard_map/split/pallas_call | solution.py:421

commit v4 on v3

--- a/solution.py
+++ b/solution.py
@@ -14,10 +14,10 @@
 TAPS, FRAME, INP, SPEC = 8, 1024, 64, 16
 NZ, NM, NG, NL = 16, 32, 8, 5
 BACK, AHEAD = 4, 3
-ROLES = [7, -7, 8] + [s * r for r in range(6, 0, -1) for s in (1, -1)] + [0]
+ROLES = [7, -7, 8, 6, -6, 5, -5, 4, -4, 2, -2, 3, -3, 1, -1, 0]
 HUB = 3
 DIRECT = 2
-CHUNKS = ((2, 4), (4, 8), (8, 12), (12, 16))
+CHUNKS = ((2, 4), (4, 7), (7, 11), (11, 16))
 
 
 def hub_of(role):

time: 117 us -> 115 us (0.983)
  the two profiles are of different devices: /device:TPU:52 before, /device:TPU:20 now
where the time goes in v4:
time: 115 us
  Pallas kernels  115 us (100%)
    pallas_call x1, Pallas kernels, shards(): packed = call(voltages, prototype, jnp.asarray(dft_table()))  112 us
    pallas_call x1, Pallas kernels, shards(): pl.pallas_call(split, out_shape=jax.ShapeDtypeStruct((1, NL, NG, 2, 64, 6...  2.6 us

profile of v4, /device:TPU:20, one launch (start us, length us, event | category | flops | bytes accessed | tf_op | source)
XLA Modules:
  0.0 115.1 jit_solution(9865693984809674573)
XLA Ops:
  0.0 112.5 %fx.1.packed = f32[8,5,64,128]{3,2,1,0:T(8,128)} custom-call(bf16[64,16,1024]{2,1,0:T(8,128)(2,1)} %volt_hbm.1, f32[8,1024]{1,0:T(8,128)} %proto.1, bf16[16,2,32,1024]{3,2,1,0:T(8,128)(2,1)} %constant.2.clone.table_hbm), custom_call_target="tpu_custom_call" | custom-call | flops 4000000000 | bytes 8000000 | tf_op jit(solution)/shard_map/fx/pallas_call | solution.py:420
  112.5 2.6 %split.1 = f32[1,5,8,2,64,64]{5,4,3,2,1,0:T(8,128)} custom-call(f32[8,5,64,128]{3,2,1,0:T(8,128)} %fx.1.packed), custom_call_target="tpu_custom_call" | custom-call | bytes 4000000 | tf_op jit(solution)/shard_map/split/pallas_call | solution.py:421
